TPU v7x, 512 devices: a whole 4x4x16 slice. The times are simulated.
512 devices in a mesh: rows: 128 (over z, y, core), cols: 4 (over x).
Axes of the slice: x: 4, y: 4, z: 16, core: 2. Of those that a mesh axis runs over, the one named last changes fastest.
Arguments:
- latent: bfloat16 [4, 128, 1024], P(None, 'rows', 'cols'), may hold values from -18 to 18
- deep: bfloat16 [320, 128, 1024], P(None, 'rows', 'cols'), may hold values from -6 to 6
- timestep: int32 [1], replicated, may hold values from 0 to 999
- in_weight: bfloat16 [36, 320], replicated, may hold values from -1 to 1
- front_weight: bfloat16 [5760, 320], P('rows'), may hold values from -0.078125 to 0.078125
- middle_weight: bfloat16 [2880, 320], P('cols'), may hold values from -0.109375 to 0.109375
- skip_weight: bfloat16 [640, 320], P('cols'), may hold values from -0.25 to 0.25
- out_weight: bfloat16 [2880, 4], replicated, may hold values from -0.109375 to 0.109375
- time_weight: bfloat16 [320, 1280], replicated, may hold values from -0.3125 to 0.3125
- time_second: bfloat16 [1280, 1280], P('cols'), may hold values from -0.15625 to 0.15625
- time_proj: bfloat16 [1280, 320], replicated, may hold values from -0.15625 to 0.15625
- input_gain: float32 [640], replicated, may hold values from 0.1 to 1.9
- middle_gain: float32 [320], replicated, may hold values from 0.1 to 1.9
- output_gain: float32 [320], replicated, may hold values from 0.1 to 1.9
Outputs:
- noise: float32 [4, 128, 1024], P(None, 'rows', 'cols')
All inputs are finite; a program needn't handle non-finite values.
Results may differ from a plain program's by a relative error of at most 0.0047.
Values may be sent and summed in bfloat16 or wider, within the bound.
No kernel may reach another device: no remote copies, remote signals or barrier semaphores. Data moves between devices by JAX's collectives and lax.ppermute only.
A program may use at most 64 MiB of HBM per device.

v0:
```python
import math
import jax
import jax.numpy as jnp
from jax import lax
from jax.sharding import Mesh
from jax.sharding import PartitionSpec as P

GROUPS = 32
ROWS = ("rows_0", "rows_1", "rows_2")
epsilon = 1e-05


def from_everyone(x, axis):
    count = lax.axis_size(axis)
    return lax.all_to_all(jnp.broadcast_to(x[None], (count, *x.shape)), axis, 0, 0, tiled=True)


def taken_together(x, axis):
    return from_everyone(x, axis).sum(axis=0)


def over_axes(x, axes):
    far, near = axes
    nearer = taken_together(x, near)
    return taken_together(nearer, far)


def together(arrays, axis):
    vector, at, finished = (jnp.concatenate([a.reshape(-1) for a in arrays]), 0, [])
    subtotal = over_axes(vector, axis)
    for a in arrays:
        finished.append(subtotal[at : at + a.size].reshape(a.shape))
        at += a.size
    return tuple(finished)


def laid_out(parts, dim):
    shape = list(parts.shape[1:])
    shape[dim] *= parts.shape[0]
    return jnp.moveaxis(parts, 0, dim).reshape(shape)


def gather_directly(x, axis, dim):
    return laid_out(from_everyone(x, axis), dim)


def padded_2(cells, sides, width):
    for axis, dim in sides:
        count = lax.axis_size(axis)
        ends = count - 1
        head = lax.slice_in_dim(cells, 0, width, axis=dim)
        tail = lax.slice_in_dim(cells, cells.shape[dim] - width, cells.shape[dim], axis=dim)
        cells = jnp.concatenate(
            [
                lax.ppermute(tail, axis, [(i, (i + 1) % count) for i in range(ends)]),
                cells,
                lax.ppermute(head, axis, [((i + 1) % count, i) for i in range(ends)]),
            ],
            axis=dim,
        )
    return cells


def unfold(padded, row_count, col_count):
    shifted = [
        padded[:, row_step : row_step + row_count, col_step : col_step + col_count]
        for row_step in range(3)
        for col_step in range(3)
    ]
    return jnp.stack(shifted, 0).reshape(9 * padded.shape[0], row_count * col_count)


def project(weight, columns):
    return lax.dot_general(
        weight, columns, (((0,), (0,)), ((), ())), preferred_element_type=jnp.float32
    )


def norm_silu(values, gain, members):
    grouped = values.reshape(GROUPS, -1)
    totals, squares = together(
        (jnp.sum(grouped, axis=1), jnp.sum(grouped * grouped, axis=1)),
        (("rows_0", "rows_1"), ("rows_2", "cols")),
    )
    center = totals / members
    offsets = grouped - center[:, None]
    spread = squares / members - center * center
    scaled = (offsets * lax.rsqrt(spread + epsilon)[:, None]).reshape(values.shape) * gain[:, None]
    return jax.nn.silu(scaled).astype(jnp.bfloat16)


def time_shift_of(timestep, time_weight, time_second, time_proj):
    half_width = time_weight.shape[0] // 2
    ratios = jnp.exp(-math.log(10000.0) * jnp.arange(half_width, dtype=jnp.float32) / half_width)
    angles = timestep[0].astype(jnp.float32) * ratios
    features = jnp.concatenate([jnp.cos(angles), jnp.sin(angles)])
    hidden = jax.nn.silu(
        jnp.dot(features, time_weight.astype(jnp.float32), precision=lax.Precision.HIGHEST)
    )
    embedded = jnp.dot(hidden, time_second.astype(jnp.float32), precision=lax.Precision.HIGHEST)
    return jnp.dot(
        jax.nn.silu(embedded), time_proj.astype(jnp.float32), precision=lax.Precision.HIGHEST
    )


def shards(
    latent,
    deep,
    timestep,
    in_weight,
    front_weight,
    middle_weight,
    skip_weight,
    out_weight,
    time_weight,
    time_second,
    time_proj,
    input_gain,
    middle_gain,
    output_gain,
):
    rows_here = latent.shape[1]
    cols_here = latent.shape[2]
    pixels = rows_here * cols_here
    image_cells = pixels * lax.axis_size(ROWS) * lax.axis_size("cols")
    channels = deep.shape[0]
    full_middle, full_skip, full_second = (
        gather_directly(middle_weight, "cols", 0),
        gather_directly(skip_weight, "cols", 0),
        gather_directly(time_second, "cols", 0),
    )
    time_shift = time_shift_of(timestep, time_weight, full_second, time_proj)
    padded_latent = padded_2(latent, ((ROWS, 1), ("cols", 2)), 1)
    skip_feat = project(in_weight, unfold(padded_latent, rows_here, cols_here)).astype(jnp.bfloat16)
    joined = jnp.concatenate([deep.reshape(channels, pixels), skip_feat], axis=0)
    members_wide = float(joined.shape[0] // GROUPS * image_cells)
    act_one = norm_silu(joined.astype(jnp.float32), input_gain, members_wide)
    padded_one = padded_2(act_one.reshape(-1, rows_here, cols_here), ((ROWS, 1), ("cols", 2)), 1)
    columns_one = unfold(padded_one, rows_here, cols_here)
    out_channels = front_weight.shape[1]
    hidden_one = project(lax.all_gather(front_weight, ROWS, axis=0, tiled=True), columns_one)
    hidden_one = hidden_one + time_shift[:, None]
    members_narrow = float(out_channels // GROUPS * image_cells)
    act_two = norm_silu(hidden_one, middle_gain, members_narrow)
    padded_two = padded_2(act_two.reshape(-1, rows_here, cols_here), ((ROWS, 1), ("cols", 2)), 1)
    block_out = project(full_middle, unfold(padded_two, rows_here, cols_here)) + project(
        full_skip, joined
    )
    act_three = norm_silu(block_out, output_gain, members_narrow)
    padded_three = padded_2(
        act_three.reshape(-1, rows_here, cols_here), ((ROWS, 1), ("cols", 2)), 1
    )
    noise = project(out_weight, unfold(padded_three, rows_here, cols_here))
    return noise.reshape(out_weight.shape[1], rows_here, cols_here)


def solution(mesh):
    finer = Mesh(
        mesh.devices.reshape(16, 4, 2, mesh.shape["cols"]), ("rows_0", "rows_1", "rows_2", "cols")
    )
    in_specs = (
        P(None, ROWS, "cols"),
        P(None, ROWS, "cols"),
        P(),
        P(),
        P(ROWS, None),
        P("cols", None),
        P("cols", None),
        P(),
        P(),
        P("cols", None),
        P(),
        P(),
        P(),
        P(),
    )
    out_specs = P(None, ROWS, "cols")
    return jax.shard_map(
        shards, mesh=finer, in_specs=in_specs, out_specs=out_specs, check_vma=False
    )
```

profile of v0, /device:TPU:25, one launch (start us, length us, event | category | flops | bytes accessed | tf_op | source)
XLA Modules:
  0.0 324.5 jit_solution(3858233901648060752)
XLA Ops:
  7.3 3.8 %collective-permute-start = (bf16[4,1,256]{2,0,1:T(4,128)(2,1)}, bf16[4,1,256]{2,0,1:T(4,128)(2,1)S(1)}, u32[]{:S(2)}, u32[]{:S(2)}) collective-permute-start(bf16[4,1,256]{2,0,1:T(4,128)(2,1)} %param.14), channel_id=1, source_target_pairs={{0,4},{4,8},{8,12},{12,16},{16,20},{20,24},{24,28},{28,32},{32,36}... | collective-permute-start | bytes 6152 | tf_op jit(solution)/shard_map/ppermute | solution.py:55
  11.0 1.9 collective-permute-start.1
  13.7 4.6 %collective-permute-done.1 = bf16[4,1,256]{2,0,1:T(4,128)(2,1)S(1)} collective-permute-done((bf16[4,1,256]{2,0,1:T(4,128)(2,1)}, bf16[4,1,256]{2,0,1:T(4,128)(2,1)S(1)}, u32[]{:S(2)}, u32[]{:S(2)}) %collective-permute-start.1) | collective-permute-done | bytes 2080 | tf_op jit(solution)/shard_map/ppermute | solution.py:57
  18.4 3.1 collective-permute-start.2
  21.5 1.3 collective-permute-start.3
  22.9 2.9 collective-permute-done.3
  27.9 1.2 convert_reduce_fusion
  29.6 8.5 %all_to_all.51 = f32[8,1,64]{2,1,0:T(1,128)S(1)} all-to-all(f32[8,1,64]{2,1,0:T(1,128)S(1)} %broadcast_in_dim.18), channel_id=1, replica_groups=mesh['rows_0'=16,'rows_1'=4,'rows_2'=2,'cols'=4] {'rows_2','cols'}, dimensions={0} | all-to-all | bytes 4096 | tf_op jit(solution)/shard_map/all_to_all | solution.py:15
  38.7 17.7 %all-to-all-start.1 = ((f32[64,1,64]{2,1,0:T(1,128)}), f32[64,1,64]{2,1,0:T(1,128)S(1)}, u32[]{:S(2)}, u32[]{:S(2)}) async-start(f32[64,1,64]{2,1,0:T(1,128)} %broadcast_in_dim.19), calls=%async_computation.1 | async-start | bytes 65536 | tf_op jit(solution)/shard_map/all_to_all | solution.py:15
  57.1 11.1 %all-to-all-done.1 = f32[64,1,64]{2,1,0:T(1,128)S(1)} async-done(((f32[64,1,64]{2,1,0:T(1,128)}), f32[64,1,64]{2,1,0:T(1,128)S(1)}, u32[]{:S(2)}, u32[]{:S(2)}) %all-to-all-start.1) | async-done | bytes 16416 | tf_op jit(solution)/shard_map/all_to_all | solution.py:15
  68.2 2.0 broadcast_in_dim.20
  70.2 4.8 %all-to-all-start.2 = ((bf16[4,320,1280]{2,1,0:T(8,128)(2,1)}), bf16[4,320,1280]{2,1,0:T(8,128)(2,1)}, u32[]{:S(2)}, u32[]{:S(2)}) async-start(bf16[4,320,1280]{2,1,0:T(8,128)(2,1)} %broadcast_in_dim.20), calls=%async_computation.2 | async-start | bytes 6553600 | tf_op jit(solution)/shard_map/all_to_all | solution.py:15
  75.8 6.3 %collective-permute-start.4 = (bf16[640,1,256]{2,0,1:T(8,128)(2,1)S(1)}, bf16[640,1,256]{2,0,1:T(8,128)(2,1)S(1)}, u32[]{:S(2)}, u32[]{:S(2)}) collective-permute-start(bf16[640,1,256]{2,0,1:T(8,128)(2,1)S(1)} %multiply_convert_fusion.1), channel_id=1, source_target_pairs={{0,4},{4,8},{8,12},{12,16},{16,20},{20,24},{24,28},{28,32},{32,36}... | collective-permute-start | bytes 983048 | tf_op jit(solution)/shard_map/ppermute | solution.py:55
  82.1 1.9 collective-permute-start.5
  84.6 1.5 collective-permute-done.4
  86.1 6.5 %collective-permute-done.5 = bf16[640,1,256]{2,0,1:T(8,128)(2,1)S(1)} collective-permute-done((bf16[640,1,256]{2,0,1:T(8,128)(2,1)S(1)}, bf16[640,1,256]{2,0,1:T(8,128)(2,1)S(1)}, u32[]{:S(2)}, u32[]{:S(2)}) %collective-permute-start.5) | collective-permute-done | bytes 327712 | tf_op jit(solution)/shard_map/ppermute | solution.py:57
  93.0 3.6 %collective-permute-start.6 = (bf16[640,3,1]{2,0,1:T(8,128)(2,1)S(1)}, bf16[640,3,1]{2,0,1:T(8,128)(2,1)S(1)}, u32[]{:S(2)}, u32[]{:S(2)}) collective-permute-start(bf16[640,3,1]{2,0,1:T(8,128)(2,1)S(1)} %get-tuple-element.12), channel_id=1, source_target_pairs={{0,1},{1,2},{2,3},{4,5},{5,6},{6,7},{8,9},{9,10},{10,11},{12,13},{... | collective-permute-start | bytes 11528 | tf_op jit(solution)/shard_map/ppermute | solution.py:55
  96.6 1.3 collective-permute-start.7
  97.9 21.1 %collective-permute-done.6 = bf16[640,3,1]{2,0,1:T(8,128)(2,1)S(1)} collective-permute-done((bf16[640,3,1]{2,0,1:T(8,128)(2,1)S(1)}, bf16[640,3,1]{2,0,1:T(8,128)(2,1)S(1)}, u32[]{:S(2)}, u32[]{:S(2)}) %collective-permute-start.6) | collective-permute-done | bytes 3872 | tf_op jit(solution)/shard_map/ppermute | solution.py:55
  127.3 3.4 %convolution_reduce_fusion = f32[1280]{0:T(1024)S(1)} fusion(f32[1280,1]{0,1:T(1,128)S(1)} %reshape.374, bf16[1280,1280]{1,0:T(8,128)(2,1)} %bitcast.27), kind=kOutput, calls=%fused_computation.3 | convolution fusion | flops 19660800 | bytes 3287040 | tf_op jit(solution)/shard_map/dot_general | solution.py:100
  131.5 25.0 %all-gather.3.cloned.1.call-done = bf16[128,45,320]{2,1,0:T(8,128)(2,1)} async-done(((bf16[1,45,320]{2,1,0:T(8,128)(2,1)}), bf16[128,45,320]{2,1,0:T(8,128)(2,1)}) %all-gather.3.cloned.1.call-update) | async-done | bytes 3686416 | tf_op jit(solution)/shard_map/all_gather | solution.py:141
  156.5 7.6 %reshape.371 = bf16[5760,320]{1,0:T(8,128)(2,1)} reshape(bf16[128,45,320]{2,1,0:T(8,128)(2,1)} %all-gather.3.cloned.1.call-done) | data formatting | bytes 7372800
  164.2 5.7 %fusion.41 = (f32[320]{0:T(512)S(1)}, f32[320]{0:T(512)S(1)}, f32[256,320]{0,1:T(8,128)}) fusion(f32[320]{0:T(512)S(1)} %convolution_reduce_fusion.2, bf16[5760,256]{1,0:T(8,128)(2,1)} %bitcast.24, bf16[5760,320]{1,0:T(8,128)(2,1)} %reshape.371), kind=kOutput, calls=%fused_computation.131 | convolution fusion | flops 944045440 | bytes 6967040 | tf_op jit(solution)/shard_map/dot_general | solution.py:74
  170.4 8.9 %all_to_all.52 = f32[8,1,64]{2,1,0:T(1,128)S(1)} all-to-all(f32[8,1,64]{2,1,0:T(1,128)S(1)} %broadcast_in_dim.21), channel_id=1, replica_groups=mesh['rows_0'=16,'rows_1'=4,'rows_2'=2,'cols'=4] {'rows_2','cols'}, dimensions={0} | all-to-all | bytes 4096 | tf_op jit(solution)/shard_map/all_to_all | solution.py:15
  180.0 3.5 %all-to-all-start.6 = ((bf16[4,160,320]{2,1,0:T(8,128)(2,1)}), bf16[4,160,320]{2,1,0:T(8,128)(2,1)S(1)}, u32[]{:S(2)}, u32[]{:S(2)}) async-start(bf16[4,160,320]{2,1,0:T(8,128)(2,1)} %broadcast_in_dim.24), calls=%async_computation.6 | async-start | bytes 983040 | tf_op jit(solution)/shard_map/all_to_all | solution.py:15
  183.5 8.5 %all-to-all-done.6 = bf16[4,160,320]{2,1,0:T(8,128)(2,1)S(1)} async-done(((bf16[4,160,320]{2,1,0:T(8,128)(2,1)}), bf16[4,160,320]{2,1,0:T(8,128)(2,1)S(1)}, u32[]{:S(2)}, u32[]{:S(2)}) %all-to-all-start.6) | async-done | bytes 409632 | tf_op jit(solution)/shard_map/all_to_all | solution.py:15
  192.0 22.1 %all_to_all.53 = f32[64,1,64]{2,1,0:T(1,128)S(1)} all-to-all(f32[64,1,64]{2,1,0:T(1,128)S(1)} %broadcast_in_dim.22), channel_id=1, replica_groups=mesh['rows_0'=16,'rows_1'=4,'rows_2'=2,'cols'=4] {'rows_0','rows_1'}, dimensions={0} | all-to-all | bytes 32768 | tf_op jit(solution)/shard_map/all_to_all | solution.py:15
  214.1 1.4 broadcast_in_dim.23
  215.5 3.7 %all-to-all-start.5 = ((bf16[4,720,320]{1,2,0:T(8,128)(2,1)}), bf16[4,720,320]{1,2,0:T(8,128)(2,1)S(1)}, u32[]{:S(2)}, u32[]{:S(2)}) async-start(bf16[4,720,320]{1,2,0:T(8,128)(2,1)} %broadcast_in_dim.23), calls=%async_computation.5 | async-start | bytes 3932160 | tf_op jit(solution)/shard_map/all_to_all | solution.py:15
  219.8 1.2 fusion.62
  221.0 7.2 %collective-permute-start.8 = (bf16[320,1,256]{2,0,1:T(8,128)(2,1)S(1)}, bf16[320,1,256]{2,0,1:T(8,128)(2,1)S(1)}, u32[]{:S(2)}, u32[]{:S(2)}) collective-permute-start(bf16[320,1,256]{2,0,1:T(8,128)(2,1)S(1)} %fusion.62), channel_id=1, source_target_pairs={{0,4},{4,8},{8,12},{12,16},{16,20},{20,24},{24,28},{28,32},{32,36}... | collective-permute-start | bytes 491528 | tf_op jit(solution)/shard_map/ppermute | solution.py:55
  228.2 1.9 collective-permute-start.9
  230.5 6.5 %collective-permute-done.9 = bf16[320,1,256]{2,0,1:T(8,128)(2,1)S(1)} collective-permute-done((bf16[320,1,256]{2,0,1:T(8,128)(2,1)S(1)}, bf16[320,1,256]{2,0,1:T(8,128)(2,1)S(1)}, u32[]{:S(2)}, u32[]{:S(2)}) %collective-permute-start.9) | collective-permute-done | bytes 163872 | tf_op jit(solution)/shard_map/ppermute | solution.py:57
  237.9 4.3 %collective-permute-start.10 = (bf16[320,3,1]{2,0,1:T(8,128)(2,1)}, bf16[320,3,1]{2,0,1:T(8,128)(2,1)}, u32[]{:S(2)}, u32[]{:S(2)}) collective-permute-start(bf16[320,3,1]{2,0,1:T(8,128)(2,1)} %get-tuple-element.16), channel_id=1, source_target_pairs={{0,1},{1,2},{2,3},{4,5},{5,6},{6,7},{8,9},{9,10},{10,11},{12,13},{... | collective-permute-start | bytes 5768 | tf_op jit(solution)/shard_map/ppermute | solution.py:55
  242.2 2.0 fusion.34
  244.2 2.8 copy.28
  247.0 3.8 %reshape.365 = bf16[2880,320]{0,1:T(8,128)(2,1)S(1)} reshape(bf16[4,720,320]{1,0,2:T(4,128)(2,1)} %copy.28) | data formatting | bytes 3686400 | tf_op jit(solution)/shard_map/reshape | solution.py:40
  250.8 1.4 collective-permute-start.11
  253.3 6.1 %collective-permute-done.11 = bf16[320,3,1]{2,0,1:T(8,128)(2,1)S(1)} collective-permute-done((bf16[320,3,1]{2,0,1:T(8,128)(2,1)S(1)}, bf16[320,3,1]{2,0,1:T(8,128)(2,1)S(1)}, u32[]{:S(2)}, u32[]{:S(2)}) %collective-permute-start.11) | collective-permute-done | bytes 1952 | tf_op jit(solution)/shard_map/ppermute | solution.py:57
  263.5 9.1 %all_to_all.54 = f32[8,1,64]{2,1,0:T(1,128)S(1)} all-to-all(f32[8,1,64]{2,1,0:T(1,128)S(1)} %broadcast_in_dim.25), channel_id=1, replica_groups=mesh['rows_0'=16,'rows_1'=4,'rows_2'=2,'cols'=4] {'rows_2','cols'}, dimensions={0} | all-to-all | bytes 4096 | tf_op jit(solution)/shard_map/all_to_all | solution.py:15
  272.6 18.1 %all_to_all.55 = f32[64,1,64]{2,1,0:T(1,128)S(1)} all-to-all(f32[64,1,64]{2,1,0:T(1,128)S(1)} %broadcast_in_dim.26), channel_id=1, replica_groups=mesh['rows_0'=16,'rows_1'=4,'rows_2'=2,'cols'=4] {'rows_0','rows_1'}, dimensions={0} | all-to-all | bytes 32768 | tf_op jit(solution)/shard_map/all_to_all | solution.py:15
  291.4 6.0 %collective-permute-start.12 = (bf16[320,1,256]{2,0,1:T(8,128)(2,1)S(1)}, bf16[320,1,256]{2,0,1:T(8,128)(2,1)S(1)}, u32[]{:S(2)}, u32[]{:S(2)}) collective-permute-start(bf16[320,1,256]{2,0,1:T(8,128)(2,1)S(1)} %fusion.61), channel_id=1, source_target_pairs={{0,4},{4,8},{8,12},{12,16},{16,20},{20,24},{24,28},{28,32},{32,36}... | collective-permute-start | bytes 491528 | tf_op jit(solution)/shard_map/ppermute | solution.py:55
  297.4 1.9 collective-permute-start.13
  299.7 6.5 %collective-permute-done.13 = bf16[320,1,256]{2,0,1:T(8,128)(2,1)S(1)} collective-permute-done((bf16[320,1,256]{2,0,1:T(8,128)(2,1)S(1)}, bf16[320,1,256]{2,0,1:T(8,128)(2,1)S(1)}, u32[]{:S(2)}, u32[]{:S(2)}) %collective-permute-start.13) | collective-permute-done | bytes 163872 | tf_op jit(solution)/shard_map/ppermute | solution.py:57
  306.4 2.2 collective-permute-start.14
  308.6 1.3 collective-permute-start.15
  309.9 1.8 collective-permute-done.14
  311.9 3.7 %collective-permute-done.15 = bf16[320,3,1]{2,0,1:T(8,128)(2,1)S(1)} collective-permute-done((bf16[320,3,1]{2,0,1:T(8,128)(2,1)S(1)}, bf16[320,3,1]{2,0,1:T(8,128)(2,1)S(1)}, u32[]{:S(2)}, u32[]{:S(2)}) %collective-permute-start.15) | collective-permute-done | bytes 1952 | tf_op jit(solution)/shard_map/ppermute | solution.py:57
  (145 shorter events, 27.3 us)
Async XLA Ops:
  6.5 77.7 %copy-start = (bf16[320,1280]{1,0:T(8,128)(2,1)S(1)}, bf16[320,1280]{1,0:T(8,128)(2,1)}, u32[]{:S(2)}) copy-start(bf16[320,1280]{1,0:T(8,128)(2,1)} %param.22) | copy-start | bytes 2457604
  6.5 61.6 %copy-start.6 = (bf16[320,1280]{1,0:T(8,128)(2,1)S(1)}, bf16[320,1280]{1,0:T(8,128)(2,1)}, u32[]{:S(2)}) copy-start(bf16[320,1280]{1,0:T(8,128)(2,1)} %param.23) | copy-start | bytes 2457604
  6.5 150.0 %all-gather.3.cloned.1.call-start = ((), (), s32[]{:S(2)}) async-start(), calls=%async_computation.9 | async-start | bytes 4755456 | tf_op jit(solution)/shard_map/all_gather | solution.py:141
  7.3 5.7 %collective-permute-start = (bf16[4,1,256]{2,0,1:T(4,128)(2,1)}, bf16[4,1,256]{2,0,1:T(4,128)(2,1)S(1)}, u32[]{:S(2)}, u32[]{:S(2)}) collective-permute-start(bf16[4,1,256]{2,0,1:T(4,128)(2,1)} %param.14), channel_id=1, source_target_pairs={{0,4},{4,8},{8,12},{12,16},{16,20},{20,24},{24,28},{28,32},{32,36}... | collective-permute-start | bytes 6152 | tf_op jit(solution)/shard_map/ppermute | solution.py:55
  11.0 7.2 %collective-permute-start.1 = (bf16[4,1,256]{2,0,1:T(4,128)(2,1)}, bf16[4,1,256]{2,0,1:T(4,128)(2,1)S(1)}, u32[]{:S(2)}, u32[]{:S(2)}) collective-permute-start(bf16[4,1,256]{2,0,1:T(4,128)(2,1)} %param.14), channel_id=1, source_target_pairs={{4,0},{8,4},{12,8},{16,12},{20,16},{24,20},{28,24},{32,28},{36,32}... | collective-permute-start | bytes 6152 | tf_op jit(solution)/shard_map/ppermute | solution.py:57
  18.4 4.4 %collective-permute-start.2 = (bf16[4,3,1]{2,0,1:T(4,128)(2,1)S(1)}, bf16[4,3,1]{2,0,1:T(4,128)(2,1)S(1)}, u32[]{:S(2)}, u32[]{:S(2)}) collective-permute-start(bf16[4,3,1]{2,0,1:T(4,128)(2,1)S(1)} %get-tuple-element.18), channel_id=1, source_target_pairs={{0,1},{1,2},{2,3},{4,5},{5,6},{6,7},{8,9},{9,10},{10,11},{12,13},{... | collective-permute-start | bytes 80 | tf_op jit(solution)/shard_map/ppermute | solution.py:55
  21.5 4.3 %collective-permute-start.3 = (bf16[4,3,1]{2,0,1:T(4,128)(2,1)S(1)}, bf16[4,3,1]{2,0,1:T(4,128)(2,1)S(1)}, u32[]{:S(2)}, u32[]{:S(2)}) collective-permute-start(bf16[4,3,1]{2,0,1:T(4,128)(2,1)S(1)} %get-tuple-element.17), channel_id=1, source_target_pairs={{1,0},{2,1},{3,2},{5,4},{6,5},{7,6},{9,8},{10,9},{11,10},{13,12},{... | collective-permute-start | bytes 80 | tf_op jit(solution)/shard_map/ppermute | solution.py:57
  38.7 29.4 %all-to-all-start.1 = ((f32[64,1,64]{2,1,0:T(1,128)}), f32[64,1,64]{2,1,0:T(1,128)S(1)}, u32[]{:S(2)}, u32[]{:S(2)}) async-start(f32[64,1,64]{2,1,0:T(1,128)} %broadcast_in_dim.19), calls=%async_computation.1 | async-start | bytes 65536 | tf_op jit(solution)/shard_map/all_to_all | solution.py:15
  70.2 5.3 %copy-start.1 = (bf16[320,1,256]{2,0,1:T(8,128)(2,1)S(1)}, bf16[320,1,256]{2,0,1:T(8,128)(2,1)}, u32[]{:S(2)}) copy-start(bf16[320,1,256]{2,0,1:T(8,128)(2,1)} %param.15) | copy-start | bytes 491524
  70.2 5.3 %copy-start.12 = (f32[640]{0:T(1024)S(1)}, f32[640]{0:T(1024)}, u32[]{:S(2)}) copy-start(f32[640]{0:T(1024)} %param.25) | copy-start | bytes 7684
  70.2 57.1 %all-to-all-start.2 = ((bf16[4,320,1280]{2,1,0:T(8,128)(2,1)}), bf16[4,320,1280]{2,1,0:T(8,128)(2,1)}, u32[]{:S(2)}, u32[]{:S(2)}) async-start(bf16[4,320,1280]{2,1,0:T(8,128)(2,1)} %broadcast_in_dim.20), calls=%async_computation.2 | async-start | bytes 6553600 | tf_op jit(solution)/shard_map/all_to_all | solution.py:15
  75.8 10.3 %collective-permute-start.4 = (bf16[640,1,256]{2,0,1:T(8,128)(2,1)S(1)}, bf16[640,1,256]{2,0,1:T(8,128)(2,1)S(1)}, u32[]{:S(2)}, u32[]{:S(2)}) collective-permute-start(bf16[640,1,256]{2,0,1:T(8,128)(2,1)S(1)} %multiply_convert_fusion.1), channel_id=1, source_target_pairs={{0,4},{4,8},{8,12},{12,16},{16,20},{20,24},{24,28},{28,32},{32,36}... | collective-permute-start | bytes 983048 | tf_op jit(solution)/shard_map/ppermute | solution.py:55
  82.1 10.5 %collective-permute-start.5 = (bf16[640,1,256]{2,0,1:T(8,128)(2,1)S(1)}, bf16[640,1,256]{2,0,1:T(8,128)(2,1)S(1)}, u32[]{:S(2)}, u32[]{:S(2)}) collective-permute-start(bf16[640,1,256]{2,0,1:T(8,128)(2,1)S(1)} %multiply_convert_fusion.1), channel_id=1, source_target_pairs={{4,0},{8,4},{12,8},{16,12},{20,16},{24,20},{28,24},{32,28},{36,32}... | collective-permute-start | bytes 983048 | tf_op jit(solution)/shard_map/ppermute | solution.py:57
  93.0 26.0 %collective-permute-start.6 = (bf16[640,3,1]{2,0,1:T(8,128)(2,1)S(1)}, bf16[640,3,1]{2,0,1:T(8,128)(2,1)S(1)}, u32[]{:S(2)}, u32[]{:S(2)}) collective-permute-start(bf16[640,3,1]{2,0,1:T(8,128)(2,1)S(1)} %get-tuple-element.12), channel_id=1, source_target_pairs={{0,1},{1,2},{2,3},{4,5},{5,6},{6,7},{8,9},{9,10},{10,11},{12,13},{... | collective-permute-start | bytes 11528 | tf_op jit(solution)/shard_map/ppermute | solution.py:55
  96.6 24.2 %collective-permute-start.7 = (bf16[640,3,1]{2,0,1:T(8,128)(2,1)S(1)}, bf16[640,3,1]{2,0,1:T(8,128)(2,1)S(1)}, u32[]{:S(2)}, u32[]{:S(2)}) collective-permute-start(bf16[640,3,1]{2,0,1:T(8,128)(2,1)S(1)} %get-tuple-element.11), channel_id=1, source_target_pairs={{1,0},{2,1},{3,2},{5,4},{6,5},{7,6},{9,8},{10,9},{11,10},{13,12},{... | collective-permute-start | bytes 11528 | tf_op jit(solution)/shard_map/ppermute | solution.py:57
  127.3 3.5 %copy-start.5 = (bf16[1280,320]{0,1:T(8,128)(2,1)S(1)}, bf16[1280,320]{0,1:T(8,128)(2,1)}, u32[]{:S(2)}) copy-start(bf16[1280,320]{0,1:T(8,128)(2,1)} %param.24) | copy-start | bytes 2457604
  164.1 15.1 %copy-start.10 = (bf16[160,320]{1,0:T(8,128)(2,1)S(1)}, bf16[160,320]{1,0:T(8,128)(2,1)}, u32[]{:S(2)}) copy-start(bf16[160,320]{1,0:T(8,128)(2,1)} %param.20) | copy-start | bytes 307204
  169.8 44.3 %copy-start.7 = (bf16[720,320]{0,1:T(8,128)(2,1)S(1)}, bf16[720,320]{0,1:T(8,128)(2,1)}, u32[]{:S(2)}) copy-start(bf16[720,320]{0,1:T(8,128)(2,1)} %param.19) | copy-start | bytes 1382404
  180.0 12.0 %all-to-all-start.6 = ((bf16[4,160,320]{2,1,0:T(8,128)(2,1)}), bf16[4,160,320]{2,1,0:T(8,128)(2,1)S(1)}, u32[]{:S(2)}, u32[]{:S(2)}) async-start(bf16[4,160,320]{2,1,0:T(8,128)(2,1)} %broadcast_in_dim.24), calls=%async_computation.6 | async-start | bytes 983040 | tf_op jit(solution)/shard_map/all_to_all | solution.py:15
  192.0 23.5 %copy-start.2 = (bf16[4,160,320]{2,1,0:T(8,128)(2,1)}, bf16[4,160,320]{2,1,0:T(8,128)(2,1)S(1)}, u32[]{:S(2)}) copy-start(bf16[4,160,320]{2,1,0:T(8,128)(2,1)S(1)} %all-to-all-done.6) | copy-start | bytes 1228804
  215.5 4.2 %copy-start.13 = (f32[320]{0:T(512)S(1)}, f32[320]{0:T(512)}, u32[]{:S(2)}) copy-start(f32[320]{0:T(512)} %param.26) | copy-start | bytes 3844
  215.5 28.7 %all-to-all-start.5 = ((bf16[4,720,320]{1,2,0:T(8,128)(2,1)}), bf16[4,720,320]{1,2,0:T(8,128)(2,1)S(1)}, u32[]{:S(2)}, u32[]{:S(2)}) async-start(bf16[4,720,320]{1,2,0:T(8,128)(2,1)} %broadcast_in_dim.23), calls=%async_computation.5 | async-start | bytes 3932160 | tf_op jit(solution)/shard_map/all_to_all | solution.py:15
  219.8 22.4 %copy-start.3 = (bf16[4,160,320]{2,1,0:T(8,128)(2,1)S(1)}, bf16[4,160,320]{2,1,0:T(8,128)(2,1)}, u32[]{:S(2)}) copy-start(bf16[4,160,320]{2,1,0:T(8,128)(2,1)} %copy-done.2) | copy-start | bytes 1228804
  221.0 9.4 %collective-permute-start.8 = (bf16[320,1,256]{2,0,1:T(8,128)(2,1)S(1)}, bf16[320,1,256]{2,0,1:T(8,128)(2,1)S(1)}, u32[]{:S(2)}, u32[]{:S(2)}) collective-permute-start(bf16[320,1,256]{2,0,1:T(8,128)(2,1)S(1)} %fusion.62), channel_id=1, source_target_pairs={{0,4},{4,8},{8,12},{12,16},{16,20},{20,24},{24,28},{28,32},{32,36}... | collective-permute-start | bytes 491528 | tf_op jit(solution)/shard_map/ppermute | solution.py:55
  228.2 8.7 %collective-permute-start.9 = (bf16[320,1,256]{2,0,1:T(8,128)(2,1)S(1)}, bf16[320,1,256]{2,0,1:T(8,128)(2,1)S(1)}, u32[]{:S(2)}, u32[]{:S(2)}) collective-permute-start(bf16[320,1,256]{2,0,1:T(8,128)(2,1)S(1)} %fusion.62), channel_id=1, source_target_pairs={{4,0},{8,4},{12,8},{16,12},{20,16},{24,20},{28,24},{32,28},{36,32}... | collective-permute-start | bytes 491528 | tf_op jit(solution)/shard_map/ppermute | solution.py:57
  237.9 14.3 %collective-permute-start.10 = (bf16[320,3,1]{2,0,1:T(8,128)(2,1)}, bf16[320,3,1]{2,0,1:T(8,128)(2,1)}, u32[]{:S(2)}, u32[]{:S(2)}) collective-permute-start(bf16[320,3,1]{2,0,1:T(8,128)(2,1)} %get-tuple-element.16), channel_id=1, source_target_pairs={{0,1},{1,2},{2,3},{4,5},{5,6},{6,7},{8,9},{9,10},{10,11},{12,13},{... | collective-permute-start | bytes 5768 | tf_op jit(solution)/shard_map/ppermute | solution.py:55
  247.0 3.8 %copy-start.9 = (bf16[320,3,1]{2,0,1:T(8,128)(2,1)S(1)}, bf16[320,3,1]{2,0,1:T(8,128)(2,1)}, u32[]{:S(2)}) copy-start(bf16[320,3,1]{2,0,1:T(8,128)(2,1)} %get-tuple-element.15) | copy-start | bytes 5764
  250.8 9.7 %copy-start.4 = (f32[256,320]{0,1:T(8,128)S(1)}, f32[256,320]{0,1:T(8,128)}, u32[]{:S(2)}) copy-start(f32[256,320]{0,1:T(8,128)} %get-tuple-element.25) | copy-start | bytes 983044
  250.8 8.6 %collective-permute-start.11 = (bf16[320,3,1]{2,0,1:T(8,128)(2,1)S(1)}, bf16[320,3,1]{2,0,1:T(8,128)(2,1)S(1)}, u32[]{:S(2)}, u32[]{:S(2)}) collective-permute-start(bf16[320,3,1]{2,0,1:T(8,128)(2,1)S(1)} %copy-done.9), channel_id=1, source_target_pairs={{1,0},{2,1},{3,2},{5,4},{6,5},{7,6},{9,8},{10,9},{11,10},{13,12},{... | collective-permute-start | bytes 5768 | tf_op jit(solution)/shard_map/ppermute | solution.py:57
  260.8 1.3 copy-start.8
  262.1 29.1 %copy-start.14 = (f32[320]{0:T(512)S(1)}, f32[320]{0:T(512)}, u32[]{:S(2)}) copy-start(f32[320]{0:T(512)} %param.27) | copy-start | bytes 3844
  291.4 8.2 %collective-permute-start.12 = (bf16[320,1,256]{2,0,1:T(8,128)(2,1)S(1)}, bf16[320,1,256]{2,0,1:T(8,128)(2,1)S(1)}, u32[]{:S(2)}, u32[]{:S(2)}) collective-permute-start(bf16[320,1,256]{2,0,1:T(8,128)(2,1)S(1)} %fusion.61), channel_id=1, source_target_pairs={{0,4},{4,8},{8,12},{12,16},{16,20},{20,24},{24,28},{28,32},{32,36}... | collective-permute-start | bytes 491528 | tf_op jit(solution)/shard_map/ppermute | solution.py:55
  297.4 8.7 %collective-permute-start.13 = (bf16[320,1,256]{2,0,1:T(8,128)(2,1)S(1)}, bf16[320,1,256]{2,0,1:T(8,128)(2,1)S(1)}, u32[]{:S(2)}, u32[]{:S(2)}) collective-permute-start(bf16[320,1,256]{2,0,1:T(8,128)(2,1)S(1)} %fusion.61), channel_id=1, source_target_pairs={{4,0},{8,4},{12,8},{16,12},{20,16},{24,20},{28,24},{32,28},{36,32}... | collective-permute-start | bytes 491528 | tf_op jit(solution)/shard_map/ppermute | solution.py:57
  306.4 5.3 %collective-permute-start.14 = (bf16[320,3,1]{2,0,1:T(8,128)(2,1)S(1)}, bf16[320,3,1]{2,0,1:T(8,128)(2,1)S(1)}, u32[]{:S(2)}, u32[]{:S(2)}) collective-permute-start(bf16[320,3,1]{2,0,1:T(8,128)(2,1)S(1)} %get-tuple-element.14), channel_id=1, source_target_pairs={{0,1},{1,2},{2,3},{4,5},{5,6},{6,7},{8,9},{9,10},{10,11},{12,13},{... | collective-permute-start | bytes 5768 | tf_op jit(solution)/shard_map/ppermute | solution.py:55
  308.6 6.9 %collective-permute-start.15 = (bf16[320,3,1]{2,0,1:T(8,128)(2,1)S(1)}, bf16[320,3,1]{2,0,1:T(8,128)(2,1)S(1)}, u32[]{:S(2)}, u32[]{:S(2)}) collective-permute-start(bf16[320,3,1]{2,0,1:T(8,128)(2,1)S(1)} %get-tuple-element.13), channel_id=1, source_target_pairs={{1,0},{2,1},{3,2},{5,4},{6,5},{7,6},{9,8},{10,9},{11,10},{13,12},{... | collective-permute-start | bytes 5768 | tf_op jit(solution)/shard_map/ppermute | solution.py:57
  316.0 0.7 copy-start.11
Sparse Core Ops, SparseCore 0:
  10.4 146.0 all-gather.2
where the time goes:
time: 326 us; the launch traced here: 325 us
  waiting for transfers between devices  107 us (33%)
  starting transfers between devices  79.1 us (24%)
  blocking collectives  66.7 us (20%)
  local copies, waits for them, and re-layouts  26.1 us (8%)
  other arithmetic  16.3 us (5%)
  between operations  14.7 us (5%)
  matrix products  14.4 us (4%)
    all_to_all x5, blocking collectives, from_everyone(): lax.all_to_all(jnp.broadcast_to(x[None], (count, *x.shape)), axis, 0, 0,...  66.7 us
    ppermute x8, waiting for transfers between devices, padded_2(): lax.ppermute(head, axis, [((i + 1) % count, i) for i in range(ends)])  37 us
    ppermute x8, starting transfers between devices, padded_2(): lax.ppermute(tail, axis, [(i, (i + 1) % count) for i in range(ends)])  36.5 us
    all_to_all x4, starting transfers between devices, from_everyone(): lax.all_to_all(jnp.broadcast_to(x[None], (count, *x.shape)), axis, 0, 0,...  29.7 us
    ppermute x8, waiting for transfers between devices, padded_2(): lax.ppermute(tail, axis, [(i, (i + 1) % count) for i in range(ends)])  25 us
    all_gather x1, waiting for transfers between devices, shards(): lax.all_gather(front_weight, ROWS, axis=0, tiled=True)  25 us
    all_to_all x4, waiting for transfers between devices, from_everyone(): lax.all_to_all(jnp.broadcast_to(x[None], (count, *x.shape)), axis, 0, 0,...  19.6 us
    ppermute x8, starting transfers between devices, padded_2(): lax.ppermute(head, axis, [((i + 1) % count, i) for i in range(ends)])  13 us
  transfers between devices with their start and end apart: 21, of which 16 were waited for; matrix products, arithmetic and copies ran while one was open for 10% of the time, Pallas kernels for 0%

commit v1 on v0

--- a/solution.py
+++ b/solution.py
@@ -138,7 +138,12 @@
     padded_one = padded_2(act_one.reshape(-1, rows_here, cols_here), ((ROWS, 1), ("cols", 2)), 1)
     columns_one = unfold(padded_one, rows_here, cols_here)
     out_channels = front_weight.shape[1]
-    hidden_one = project(lax.all_gather(front_weight, ROWS, axis=0, tiled=True), columns_one)
+    hidden_one = project(
+        jnp.concatenate(
+            lax.all_to_all(jnp.stack([front_weight] * lax.axis_size(ROWS)), ROWS, 0, 0), axis=0
+        ),
+        columns_one,
+    )
     hidden_one = hidden_one + time_shift[:, None]
     members_narrow = float(out_channels // GROUPS * image_cells)
     act_two = norm_silu(hidden_one, middle_gain, members_narrow)

time: 326 us -> 508 us (1.56)
  waiting for transfers between devices: 107 us -> 249 us
  blocking collectives: 66.7 us -> 140 us
  starting transfers between devices: 79.1 us -> 64.3 us
  between operations: 14.7 us -> 1.38 us
  other arithmetic: 16.3 us -> 11.1 us
    ppermute x8, waiting for transfers between devices: 25 us -> 204 us  [padded_2(): lax.ppermute(tail, axis, [(i, (i + 1) % count) for i in range(ends)])]
    all_to_all x5 -> x7, blocking collectives: 66.7 us -> 140 us  [from_everyone(): lax.all_to_all(jnp.broadcast_to(x[None], (count, *x.shape)), axis, 0, 0,...]
    all_gather x1 -> x0, waiting for transfers between devices: 25 us -> none  [shards(): lax.all_gather(front_weight, ROWS, axis=0, tiled=True)]
    all_to_all x4 -> x2, starting transfers between devices: 29.7 us -> 7.2 us  [from_everyone(): lax.all_to_all(jnp.broadcast_to(x[None], (count, *x.shape)), axis, 0, 0,...]
    all_to_all x0 -> x1, starting transfers between devices: none -> 11.6 us  [shards(): lax.all_to_all(jnp.stack([front_weight] * lax.axis_size(ROWS)), ROWS, 0, 0)]
    all_to_all x4 -> x2, waiting for transfers between devices: 19.6 us -> 8.47 us  [from_everyone(): lax.all_to_all(jnp.broadcast_to(x[None], (count, *x.shape)), axis, 0, 0,...]
    reshape x0 -> x1, local copies, waits for them, and re-layouts: none -> 7.64 us  [shards(): jnp.concatenate(lax.all_to_all(jnp.stack([front_weight] * lax.axis_size(R...]
    unnamed x42 -> x45, local copies, waits for them, and re-layouts: 11 us -> 4.45 us
  transfers between devices with their start and end apart: 21 -> 19, of which waited for: 16 -> 14; matrix products, arithmetic and copies ran while one was open for 10% -> 4% of each run, Pallas kernels for 0% -> 0%
where the time goes in v1:
time: 508 us; the launch traced here: 507 us
  waiting for transfers between devices  249 us (49%)
  blocking collectives  140 us (28%)
  starting transfers between devices  64.3 us (13%)
  local copies, waits for them, and re-layouts  28.6 us (6%)
  matrix products  12.4 us (2%)
  other arithmetic  11.1 us (2%)
    ppermute x8, waiting for transfers between devices, padded_2(): lax.ppermute(tail, axis, [(i, (i + 1) % count) for i in range(ends)])  204 us
    all_to_all x7, blocking collectives, from_everyone(): lax.all_to_all(jnp.broadcast_to(x[None], (count, *x.shape)), axis, 0, 0,...  140 us
    ppermute x8, waiting for transfers between devices, padded_2(): lax.ppermute(head, axis, [((i + 1) % count, i) for i in range(ends)])  36 us
    ppermute x8, starting transfers between devices, padded_2(): lax.ppermute(tail, axis, [(i, (i + 1) % count) for i in range(ends)])  32.1 us
    ppermute x8, starting transfers between devices, padded_2(): lax.ppermute(head, axis, [((i + 1) % count, i) for i in range(ends)])  13.4 us
    all_to_all x1, starting transfers between devices, shards(): lax.all_to_all(jnp.stack([front_weight] * lax.axis_size(ROWS)), ROWS, 0, 0)  11.6 us
  transfers between devices with their start and end apart: 19, of which 14 were waited for; matrix products, arithmetic and copies ran while one was open for 4% of the time, Pallas kernels for 0%

profile of v1, /device:TPU:25, one launch (start us, length us, event | category | flops | bytes accessed | tf_op | source)
XLA Modules:
  0.0 506.6 jit_solution(2787025349475000043)
XLA Ops:
  0.0 3.9 collective-permute-start
  3.9 1.9 collective-permute-start.1
  6.5 4.6 collective-permute-done.1
  11.2 3.1 collective-permute-start.2
  14.3 1.3 collective-permute-start.3
  15.7 2.9 collective-permute-done.3
  22.5 8.5 %all_to_all.56 = f32[8,1,64]{2,1,0:T(1,128)S(1)} all-to-all(f32[8,1,64]{2,1,0:T(1,128)S(1)} %broadcast_in_dim.18), channel_id=1, replica_groups=mesh['rows_0'=16,'rows_1'=4,'rows_2'=2,'cols'=4] {'rows_2','cols'}, dimensions={0} | all-to-all | bytes 4096 | tf_op jit(solution)/shard_map/all_to_all | solution.py:15
  31.0 29.2 %all_to_all.57 = f32[64,1,64]{2,1,0:T(1,128)S(1)} all-to-all(f32[64,1,64]{2,1,0:T(1,128)S(1)} %broadcast_in_dim.19), channel_id=1, replica_groups=mesh['rows_0'=16,'rows_1'=4,'rows_2'=2,'cols'=4] {'rows_0','rows_1'}, dimensions={0} | all-to-all | bytes 32768 | tf_op jit(solution)/shard_map/all_to_all | solution.py:15
  60.3 1.4 broadcast_in_dim.20
  61.6 40.1 %all_to_all.58 = bf16[4,320,1280]{2,1,0:T(8,128)(2,1)} all-to-all(bf16[4,320,1280]{2,1,0:T(8,128)(2,1)S(1)} %broadcast_in_dim.20), channel_id=1, replica_groups=mesh['rows_0'=16,'rows_1'=4,'rows_2'=2,'cols'=4] {'cols'}, dimensions={0} | all-to-all | bytes 6553600 | tf_op jit(solution)/shard_map/all_to_all | solution.py:15
  101.7 2.6 stack.95
  104.3 11.6 %all-to-all-start.2 = ((bf16[128,45,320]{2,1,0:T(8,128)(2,1)}), bf16[128,45,320]{2,1,0:T(8,128)(2,1)}, u32[]{:S(2)}, u32[]{:S(2)}) async-start(bf16[128,45,320]{2,1,0:T(8,128)(2,1)} %stack.95), calls=%async_computation.2 | async-start | bytes 9437184 | tf_op jit(solution)/shard_map/all_to_all | solution.py:143
  117.4 3.4 collective-permute-start.4
  120.8 1.9 collective-permute-start.5
  123.3 197.5 %collective-permute-done.4 = bf16[640,1,256]{2,0,1:T(8,128)(2,1)S(1)} collective-permute-done((bf16[640,1,256]{2,0,1:T(8,128)(2,1)S(1)}, bf16[640,1,256]{2,0,1:T(8,128)(2,1)S(1)}, u32[]{:S(2)}, u32[]{:S(2)}) %collective-permute-start.4) | collective-permute-done | bytes 327712 | tf_op jit(solution)/shard_map/ppermute | solution.py:55
  320.7 2.4 collective-permute-done.5
  323.5 2.2 collective-permute-start.6
  325.8 1.5 collective-permute-start.7
  327.3 4.2 collective-permute-done.6
  331.7 3.7 collective-permute-done.7
  336.7 2.6 copy-done.1
  339.3 1.4 convolution_reduce_fusion
  341.5 7.6 %reshape.367 = bf16[5760,320]{1,0:T(8,128)(2,1)} reshape(bf16[128,45,320]{2,1,0:T(8,128)(2,1)} %all-to-all-done.2) | data formatting | bytes 7372800 | tf_op jit(solution)/shard_map/reshape | solution.py:142
  349.2 5.7 %fusion.41 = (f32[320]{0:T(512)S(1)}, f32[320]{0:T(512)S(1)}, f32[256,320]{0,1:T(8,128)}) fusion(f32[320]{0:T(512)S(1)} %convolution_reduce_fusion.2, bf16[5760,256]{1,0:T(8,128)(2,1)} %bitcast.211, bf16[5760,320]{1,0:T(8,128)(2,1)} %reshape.367), kind=kOutput, calls=%fused_computation.131 | convolution fusion | flops 944045440 | bytes 6967040 | tf_op jit(solution)/shard_map/dot_general | solution.py:74
  355.4 7.8 %all_to_all.59 = f32[8,1,64]{2,1,0:T(1,128)S(1)} all-to-all(f32[8,1,64]{2,1,0:T(1,128)S(1)} %broadcast_in_dim.21), channel_id=1, replica_groups=mesh['rows_0'=16,'rows_1'=4,'rows_2'=2,'cols'=4] {'rows_2','cols'}, dimensions={0} | all-to-all | bytes 4096 | tf_op jit(solution)/shard_map/all_to_all | solution.py:15
  364.0 3.5 all-to-all-start.7
  367.5 8.5 %all-to-all-done.7 = bf16[4,160,320]{2,1,0:T(8,128)(2,1)S(1)} async-done(((bf16[4,160,320]{2,1,0:T(8,128)(2,1)}), bf16[4,160,320]{2,1,0:T(8,128)(2,1)S(1)}, u32[]{:S(2)}, u32[]{:S(2)}) %all-to-all-start.7) | async-done | bytes 409632 | tf_op jit(solution)/shard_map/all_to_all | solution.py:15
  376.0 27.0 %all_to_all.60 = f32[64,1,64]{2,1,0:T(1,128)S(1)} all-to-all(f32[64,1,64]{2,1,0:T(1,128)S(1)} %broadcast_in_dim.22), channel_id=1, replica_groups=mesh['rows_0'=16,'rows_1'=4,'rows_2'=2,'cols'=4] {'rows_0','rows_1'}, dimensions={0} | all-to-all | bytes 32768 | tf_op jit(solution)/shard_map/all_to_all | solution.py:15
  403.0 1.4 broadcast_in_dim.23
  404.4 3.7 all-to-all-start.6
  409.9 7.0 %collective-permute-start.8 = (bf16[320,1,256]{2,0,1:T(8,128)(2,1)S(1)}, bf16[320,1,256]{2,0,1:T(8,128)(2,1)S(1)}, u32[]{:S(2)}, u32[]{:S(2)}) collective-permute-start(bf16[320,1,256]{2,0,1:T(8,128)(2,1)S(1)} %fusion.62), channel_id=1, source_target_pairs={{0,4},{4,8},{8,12},{12,16},{16,20},{20,24},{24,28},{28,32},{32,36}... | collective-permute-start | bytes 491528 | tf_op jit(solution)/shard_map/ppermute | solution.py:55
  416.9 1.9 collective-permute-start.9
  419.1 6.5 %collective-permute-done.9 = bf16[320,1,256]{2,0,1:T(8,128)(2,1)S(1)} collective-permute-done((bf16[320,1,256]{2,0,1:T(8,128)(2,1)S(1)}, bf16[320,1,256]{2,0,1:T(8,128)(2,1)S(1)}, u32[]{:S(2)}, u32[]{:S(2)}) %collective-permute-start.9) | collective-permute-done | bytes 163872 | tf_op jit(solution)/shard_map/ppermute | solution.py:57
  426.6 4.3 collective-permute-start.10
  430.9 2.0 fusion.34
  432.9 2.8 copy.28
  435.7 3.8 reshape.371
  439.5 1.6 collective-permute-start.11
  442.2 5.7 %collective-permute-done.11 = bf16[320,3,1]{2,0,1:T(8,128)(2,1)S(1)} collective-permute-done((bf16[320,3,1]{2,0,1:T(8,128)(2,1)S(1)}, bf16[320,3,1]{2,0,1:T(8,128)(2,1)S(1)}, u32[]{:S(2)}, u32[]{:S(2)}) %collective-permute-start.11) | collective-permute-done | bytes 1952 | tf_op jit(solution)/shard_map/ppermute | solution.py:57
  451.9 9.6 %all_to_all.61 = f32[8,1,64]{2,1,0:T(1,128)S(1)} all-to-all(f32[8,1,64]{2,1,0:T(1,128)S(1)} %broadcast_in_dim.25), channel_id=1, replica_groups=mesh['rows_0'=16,'rows_1'=4,'rows_2'=2,'cols'=4] {'rows_2','cols'}, dimensions={0} | all-to-all | bytes 4096 | tf_op jit(solution)/shard_map/all_to_all | solution.py:15
  461.5 18.0 %all_to_all.62 = f32[64,1,64]{2,1,0:T(1,128)S(1)} all-to-all(f32[64,1,64]{2,1,0:T(1,128)S(1)} %broadcast_in_dim.26), channel_id=1, replica_groups=mesh['rows_0'=16,'rows_1'=4,'rows_2'=2,'cols'=4] {'rows_0','rows_1'}, dimensions={0} | all-to-all | bytes 32768 | tf_op jit(solution)/shard_map/all_to_all | solution.py:15
  480.3 6.0 %collective-permute-start.12 = (bf16[320,1,256]{2,0,1:T(8,128)(2,1)S(1)}, bf16[320,1,256]{2,0,1:T(8,128)(2,1)S(1)}, u32[]{:S(2)}, u32[]{:S(2)}) collective-permute-start(bf16[320,1,256]{2,0,1:T(8,128)(2,1)S(1)} %fusion.61), channel_id=1, source_target_pairs={{0,4},{4,8},{8,12},{12,16},{16,20},{20,24},{24,28},{28,32},{32,36}... | collective-permute-start | bytes 491528 | tf_op jit(solution)/shard_map/ppermute | solution.py:55
  486.3 1.9 collective-permute-start.13
  488.5 6.5 %collective-permute-done.13 = bf16[320,1,256]{2,0,1:T(8,128)(2,1)S(1)} collective-permute-done((bf16[320,1,256]{2,0,1:T(8,128)(2,1)S(1)}, bf16[320,1,256]{2,0,1:T(8,128)(2,1)S(1)}, u32[]{:S(2)}, u32[]{:S(2)}) %collective-permute-start.13) | collective-permute-done | bytes 163872 | tf_op jit(solution)/shard_map/ppermute | solution.py:57
  495.2 2.2 collective-permute-start.14
  497.5 1.3 collective-permute-start.15
  498.8 1.8 collective-permute-done.14
  500.7 3.7 collective-permute-done.15
  (147 shorter events, 21.5 us)
Async XLA Ops:
  0.0 122.8 %copy-start = (bf16[320,1280]{1,0:T(8,128)(2,1)S(1)}, bf16[320,1280]{1,0:T(8,128)(2,1)}, u32[]{:S(2)}) copy-start(bf16[320,1280]{1,0:T(8,128)(2,1)} %param.22) | copy-start | bytes 2457604
  0.0 5.8 %collective-permute-start = (bf16[4,1,256]{2,0,1:T(4,128)(2,1)}, bf16[4,1,256]{2,0,1:T(4,128)(2,1)S(1)}, u32[]{:S(2)}, u32[]{:S(2)}) collective-permute-start(bf16[4,1,256]{2,0,1:T(4,128)(2,1)} %param.14), channel_id=1, source_target_pairs={{0,4},{4,8},{8,12},{12,16},{16,20},{20,24},{24,28},{28,32},{32,36}... | collective-permute-start | bytes 6152 | tf_op jit(solution)/shard_map/ppermute | solution.py:55
  3.9 7.2 %collective-permute-start.1 = (bf16[4,1,256]{2,0,1:T(4,128)(2,1)}, bf16[4,1,256]{2,0,1:T(4,128)(2,1)S(1)}, u32[]{:S(2)}, u32[]{:S(2)}) collective-permute-start(bf16[4,1,256]{2,0,1:T(4,128)(2,1)} %param.14), channel_id=1, source_target_pairs={{4,0},{8,4},{12,8},{16,12},{20,16},{24,20},{28,24},{32,28},{36,32}... | collective-permute-start | bytes 6152 | tf_op jit(solution)/shard_map/ppermute | solution.py:57
  11.2 4.4 collective-permute-start.2
  14.3 4.3 collective-permute-start.3
  61.6 40.1 %copy-start.11 = (bf16[45,320]{1,0:T(8,128)(2,1)S(1)}, bf16[45,320]{1,0:T(8,128)(2,1)}, u32[]{:S(2)}) copy-start(bf16[45,320]{1,0:T(8,128)(2,1)} %param.18) | copy-start | bytes 86404
  104.3 12.8 %copy-start.2 = (bf16[320,1,256]{2,0,1:T(8,128)(2,1)S(1)}, bf16[320,1,256]{2,0,1:T(8,128)(2,1)}, u32[]{:S(2)}) copy-start(bf16[320,1,256]{2,0,1:T(8,128)(2,1)} %param.15) | copy-start | bytes 491524
  104.3 12.8 %copy-start.14 = (f32[640]{0:T(1024)S(1)}, f32[640]{0:T(1024)}, u32[]{:S(2)}) copy-start(f32[640]{0:T(1024)} %param.25) | copy-start | bytes 7684
  104.3 237.3 %all-to-all-start.2 = ((bf16[128,45,320]{2,1,0:T(8,128)(2,1)}), bf16[128,45,320]{2,1,0:T(8,128)(2,1)}, u32[]{:S(2)}, u32[]{:S(2)}) async-start(bf16[128,45,320]{2,1,0:T(8,128)(2,1)} %stack.95), calls=%async_computation.2 | async-start | bytes 9437184 | tf_op jit(solution)/shard_map/all_to_all | solution.py:143
  117.4 203.3 %collective-permute-start.4 = (bf16[640,1,256]{2,0,1:T(8,128)(2,1)S(1)}, bf16[640,1,256]{2,0,1:T(8,128)(2,1)S(1)}, u32[]{:S(2)}, u32[]{:S(2)}) collective-permute-start(bf16[640,1,256]{2,0,1:T(8,128)(2,1)S(1)} %multiply_convert_fusion.1), channel_id=1, source_target_pairs={{0,4},{4,8},{8,12},{12,16},{16,20},{20,24},{24,28},{28,32},{32,36}... | collective-permute-start | bytes 983048 | tf_op jit(solution)/shard_map/ppermute | solution.py:55
  120.8 202.4 %collective-permute-start.5 = (bf16[640,1,256]{2,0,1:T(8,128)(2,1)S(1)}, bf16[640,1,256]{2,0,1:T(8,128)(2,1)S(1)}, u32[]{:S(2)}, u32[]{:S(2)}) collective-permute-start(bf16[640,1,256]{2,0,1:T(8,128)(2,1)S(1)} %multiply_convert_fusion.1), channel_id=1, source_target_pairs={{4,0},{8,4},{12,8},{16,12},{20,16},{24,20},{28,24},{32,28},{36,32}... | collective-permute-start | bytes 983048 | tf_op jit(solution)/shard_map/ppermute | solution.py:57
  323.5 8.0 %collective-permute-start.6 = (bf16[640,3,1]{2,0,1:T(8,128)(2,1)S(1)}, bf16[640,3,1]{2,0,1:T(8,128)(2,1)S(1)}, u32[]{:S(2)}, u32[]{:S(2)}) collective-permute-start(bf16[640,3,1]{2,0,1:T(8,128)(2,1)S(1)} %get-tuple-element.12), channel_id=1, source_target_pairs={{0,1},{1,2},{2,3},{4,5},{5,6},{6,7},{8,9},{9,10},{10,11},{12,13},{... | collective-permute-start | bytes 11528 | tf_op jit(solution)/shard_map/ppermute | solution.py:55
  325.8 9.6 %collective-permute-start.7 = (bf16[640,3,1]{2,0,1:T(8,128)(2,1)S(1)}, bf16[640,3,1]{2,0,1:T(8,128)(2,1)S(1)}, u32[]{:S(2)}, u32[]{:S(2)}) collective-permute-start(bf16[640,3,1]{2,0,1:T(8,128)(2,1)S(1)} %get-tuple-element.11), channel_id=1, source_target_pairs={{1,0},{2,1},{3,2},{5,4},{6,5},{7,6},{9,8},{10,9},{11,10},{13,12},{... | collective-permute-start | bytes 11528 | tf_op jit(solution)/shard_map/ppermute | solution.py:57
  336.3 3.0 copy-start.1
  336.7 4.0 copy-start.12
  339.3 1.5 copy-start.6
  349.2 14.0 %copy-start.10 = (bf16[160,320]{1,0:T(8,128)(2,1)S(1)}, bf16[160,320]{1,0:T(8,128)(2,1)}, u32[]{:S(2)}) copy-start(bf16[160,320]{1,0:T(8,128)(2,1)} %param.20) | copy-start | bytes 307204
  354.8 48.1 %copy-start.7 = (bf16[720,320]{0,1:T(8,128)(2,1)S(1)}, bf16[720,320]{0,1:T(8,128)(2,1)}, u32[]{:S(2)}) copy-start(bf16[720,320]{0,1:T(8,128)(2,1)} %param.19) | copy-start | bytes 1382404
  364.0 12.0 %all-to-all-start.7 = ((bf16[4,160,320]{2,1,0:T(8,128)(2,1)}), bf16[4,160,320]{2,1,0:T(8,128)(2,1)S(1)}, u32[]{:S(2)}, u32[]{:S(2)}) async-start(bf16[4,160,320]{2,1,0:T(8,128)(2,1)} %broadcast_in_dim.24), calls=%async_computation.7 | async-start | bytes 983040 | tf_op jit(solution)/shard_map/all_to_all | solution.py:15
  375.9 28.4 %copy-start.3 = (bf16[4,160,320]{2,1,0:T(8,128)(2,1)}, bf16[4,160,320]{2,1,0:T(8,128)(2,1)S(1)}, u32[]{:S(2)}) copy-start(bf16[4,160,320]{2,1,0:T(8,128)(2,1)S(1)} %all-to-all-done.7) | copy-start | bytes 1228804
  404.4 4.2 copy-start.15
  404.4 28.5 %all-to-all-start.6 = ((bf16[4,720,320]{1,2,0:T(8,128)(2,1)}), bf16[4,720,320]{1,2,0:T(8,128)(2,1)S(1)}, u32[]{:S(2)}, u32[]{:S(2)}) async-start(bf16[4,720,320]{1,2,0:T(8,128)(2,1)} %broadcast_in_dim.23), calls=%async_computation.6 | async-start | bytes 3932160 | tf_op jit(solution)/shard_map/all_to_all | solution.py:15
  408.6 22.3 %copy-start.4 = (bf16[4,160,320]{2,1,0:T(8,128)(2,1)S(1)}, bf16[4,160,320]{2,1,0:T(8,128)(2,1)}, u32[]{:S(2)}) copy-start(bf16[4,160,320]{2,1,0:T(8,128)(2,1)} %copy-done.3) | copy-start | bytes 1228804
  409.9 9.2 %collective-permute-start.8 = (bf16[320,1,256]{2,0,1:T(8,128)(2,1)S(1)}, bf16[320,1,256]{2,0,1:T(8,128)(2,1)S(1)}, u32[]{:S(2)}, u32[]{:S(2)}) collective-permute-start(bf16[320,1,256]{2,0,1:T(8,128)(2,1)S(1)} %fusion.62), channel_id=1, source_target_pairs={{0,4},{4,8},{8,12},{12,16},{16,20},{20,24},{24,28},{28,32},{32,36}... | collective-permute-start | bytes 491528 | tf_op jit(solution)/shard_map/ppermute | solution.py:55
  416.9 8.7 %collective-permute-start.9 = (bf16[320,1,256]{2,0,1:T(8,128)(2,1)S(1)}, bf16[320,1,256]{2,0,1:T(8,128)(2,1)S(1)}, u32[]{:S(2)}, u32[]{:S(2)}) collective-permute-start(bf16[320,1,256]{2,0,1:T(8,128)(2,1)S(1)} %fusion.62), channel_id=1, source_target_pairs={{4,0},{8,4},{12,8},{16,12},{20,16},{24,20},{28,24},{32,28},{36,32}... | collective-permute-start | bytes 491528 | tf_op jit(solution)/shard_map/ppermute | solution.py:57
  426.6 14.6 %collective-permute-start.10 = (bf16[320,3,1]{2,0,1:T(8,128)(2,1)}, bf16[320,3,1]{2,0,1:T(8,128)(2,1)}, u32[]{:S(2)}, u32[]{:S(2)}) collective-permute-start(bf16[320,3,1]{2,0,1:T(8,128)(2,1)} %get-tuple-element.16), channel_id=1, source_target_pairs={{0,1},{1,2},{2,3},{4,5},{5,6},{6,7},{8,9},{9,10},{10,11},{12,13},{... | collective-permute-start | bytes 5768 | tf_op jit(solution)/shard_map/ppermute | solution.py:55
  435.7 3.8 copy-start.9
  439.5 9.5 %copy-start.5 = (f32[256,320]{0,1:T(8,128)S(1)}, f32[256,320]{0,1:T(8,128)}, u32[]{:S(2)}) copy-start(f32[256,320]{0,1:T(8,128)} %get-tuple-element.25) | copy-start | bytes 983044
  439.5 8.4 %collective-permute-start.11 = (bf16[320,3,1]{2,0,1:T(8,128)(2,1)S(1)}, bf16[320,3,1]{2,0,1:T(8,128)(2,1)S(1)}, u32[]{:S(2)}, u32[]{:S(2)}) collective-permute-start(bf16[320,3,1]{2,0,1:T(8,128)(2,1)S(1)} %copy-done.9), channel_id=1, source_target_pairs={{1,0},{2,1},{3,2},{5,4},{6,5},{7,6},{9,8},{10,9},{11,10},{13,12},{... | collective-permute-start | bytes 5768 | tf_op jit(solution)/shard_map/ppermute | solution.py:57
  449.2 1.3 copy-start.8
  450.6 29.5 %copy-start.16 = (f32[320]{0:T(512)S(1)}, f32[320]{0:T(512)}, u32[]{:S(2)}) copy-start(f32[320]{0:T(512)} %param.27) | copy-start | bytes 3844
  480.3 8.2 %collective-permute-start.12 = (bf16[320,1,256]{2,0,1:T(8,128)(2,1)S(1)}, bf16[320,1,256]{2,0,1:T(8,128)(2,1)S(1)}, u32[]{:S(2)}, u32[]{:S(2)}) collective-permute-start(bf16[320,1,256]{2,0,1:T(8,128)(2,1)S(1)} %fusion.61), channel_id=1, source_target_pairs={{0,4},{4,8},{8,12},{12,16},{16,20},{20,24},{24,28},{28,32},{32,36}... | collective-permute-start | bytes 491528 | tf_op jit(solution)/shard_map/ppermute | solution.py:55
  486.3 8.7 %collective-permute-start.13 = (bf16[320,1,256]{2,0,1:T(8,128)(2,1)S(1)}, bf16[320,1,256]{2,0,1:T(8,128)(2,1)S(1)}, u32[]{:S(2)}, u32[]{:S(2)}) collective-permute-start(bf16[320,1,256]{2,0,1:T(8,128)(2,1)S(1)} %fusion.61), channel_id=1, source_target_pairs={{4,0},{8,4},{12,8},{16,12},{20,16},{24,20},{28,24},{32,28},{36,32}... | collective-permute-start | bytes 491528 | tf_op jit(solution)/shard_map/ppermute | solution.py:57
  495.2 5.3 %collective-permute-start.14 = (bf16[320,3,1]{2,0,1:T(8,128)(2,1)S(1)}, bf16[320,3,1]{2,0,1:T(8,128)(2,1)S(1)}, u32[]{:S(2)}, u32[]{:S(2)}) collective-permute-start(bf16[320,3,1]{2,0,1:T(8,128)(2,1)S(1)} %get-tuple-element.14), channel_id=1, source_target_pairs={{0,1},{1,2},{2,3},{4,5},{5,6},{6,7},{8,9},{9,10},{10,11},{12,13},{... | collective-permute-start | bytes 5768 | tf_op jit(solution)/shard_map/ppermute | solution.py:55
  497.5 6.9 %collective-permute-start.15 = (bf16[320,3,1]{2,0,1:T(8,128)(2,1)S(1)}, bf16[320,3,1]{2,0,1:T(8,128)(2,1)S(1)}, u32[]{:S(2)}, u32[]{:S(2)}) collective-permute-start(bf16[320,3,1]{2,0,1:T(8,128)(2,1)S(1)} %get-tuple-element.13), channel_id=1, source_target_pairs={{1,0},{2,1},{3,2},{5,4},{6,5},{7,6},{9,8},{10,9},{11,10},{13,12},{... | collective-permute-start | bytes 5768 | tf_op jit(solution)/shard_map/ppermute | solution.py:57
  504.9 0.7 copy-start.13
